TPU v7x, 32 devices: a whole 2x2x4 slice. The times are simulated.
32 devices in a mesh: row: 4 (over y, core), col: 8 (over z, x).
Axes of the slice: x: 2, y: 2, z: 4, core: 2. Of those that a mesh axis runs over, the one named last changes fastest.
Arguments:
- features: bfloat16 [4096, 128], P(('row', 'col')), may hold values from -6 to 6
- norm_weight: float32 [4096], P(('row', 'col')), may hold values from 0.01767767 to 0.110485435
- weight_in: bfloat16 [128, 256], replicated, may hold values from -6 to 6
- weight_out: bfloat16 [256, 128], replicated, may hold values from -6 to 6
- labels: int32 [4096], P(('row', 'col')), may hold values from 0 to 127
- tile_slot: int32 [32, 128], P(('row', 'col')), may hold values from 0 to 31
- tile_edges: int32 [32, 128, 2, 512], P(('row', 'col')), may hold values from 0 to 127
- tile_count: int32 [32], P(('row', 'col')), may hold values from 32 to 128, as said below
Outputs:
- grad_in: float32 [128, 256], replicated
- grad_out: float32 [256, 128], replicated
- loss: float32 [], replicated
Inputs may be any that keep to these rules, and one draw needn't show every extreme that they name: `tile_slot`: position p of a slot covers the tile whose target rows start at 128 * (p // 4) and whose source columns start at 128 * (p % 4) within the device's block; a position may occur in several slots. Entry k of a slot marks row tile_edges[s, 0, k] and column tile_edges[s, 1, k] of its slot's tile; repeated entries count again. `tile_count`: slots at and after this number are not live; in every draw some device has all 128 slots live and another device only 32.
All inputs are finite; a program needn't handle non-finite values.
Results may differ from a plain program's by a relative error of at most 0.0084.
Values may be sent and summed in bfloat16 or wider, within the bound.
A program may use at most 64 MiB of HBM per device.

v0:
```python
import jax
import jax.numpy as jnp
from jax import lax
from jax.sharding import PartitionSpec as P

TILE = 128
SOFTCAP = 15.0
LOSS_SCALE = 1024.0
HIGHEST = lax.Precision.HIGHEST
CONTRACT_ROWS = (((0,), (0,)), ((), ()))


def densify(tile_slot, tile_edges, tile_count, row_group, col_group):
    tile_side = TILE
    col_tiles = col_group // tile_side
    row_tiles = row_group // tile_side
    slot_total = tile_slot.shape[0]
    offsets = jnp.arange(tile_side, dtype=jnp.int32)
    row_onehot = (tile_edges[:, 0, :, None] == offsets[None, None, :]).astype(jnp.bfloat16)
    col_onehot = (tile_edges[:, 1, :, None] == offsets[None, None, :]).astype(jnp.bfloat16)
    slot_tiles = jnp.einsum(
        "ser,sec->src", row_onehot, col_onehot, preferred_element_type=jnp.float32
    )
    slot_tiles = slot_tiles.astype(jnp.bfloat16).reshape(slot_total, tile_side * tile_side)
    slot_live = jnp.arange(slot_total, dtype=jnp.int32) < tile_count
    places = jnp.arange(row_tiles * col_tiles, dtype=jnp.int32)
    place_onehot = ((tile_slot[:, None] == places[None, :]) & slot_live[:, None]).astype(
        jnp.bfloat16
    )
    placed = lax.dot_general(
        place_onehot, slot_tiles, CONTRACT_ROWS, preferred_element_type=jnp.float32
    )
    placed = placed.astype(jnp.bfloat16).reshape(row_tiles, col_tiles, tile_side, tile_side)
    return placed.transpose(0, 2, 1, 3).reshape(row_group, col_group)


def gather_targets(values):
    return lax.all_gather(values, "col", axis=0, tiled=True)


def sum_sources(partial_sums):
    return lax.psum_scatter(partial_sums, "row", scatter_dimension=0, tiled=True)


def per_device(
    features, norm_weight, weight_in, weight_out, labels, tile_slot, tile_edges, tile_count
):
    row_size = lax.axis_size("row")
    col_size = lax.axis_size("col")
    node_rows = features.shape[0]
    total_nodes = node_rows * row_size * col_size
    adjacency = densify(
        tile_slot[0], tile_edges[0], tile_count[0], node_rows * col_size, node_rows * row_size
    )
    node_scale = norm_weight[:, None]
    normed = (node_scale * features.astype(jnp.float32)).astype(jnp.bfloat16)
    source_one = jnp.dot(normed, weight_in, preferred_element_type=jnp.float32)
    gathered_one = lax.all_gather(source_one, "row", axis=0, tiled=True)
    forward_one = jnp.dot(adjacency.astype(jnp.float32), gathered_one, precision=HIGHEST)
    projected = lax.psum_scatter(forward_one, "col", scatter_dimension=0, tiled=True)
    pre_hidden = node_scale * (projected + source_one)
    hidden = jax.nn.relu(pre_hidden).astype(jnp.bfloat16)
    source_two = (
        node_scale * jnp.dot(hidden, weight_out, preferred_element_type=jnp.float32)
    ).astype(jnp.bfloat16)
    gathered_two = lax.all_gather(source_two, "row", axis=0, tiled=True)
    forward_two = jnp.dot(adjacency, gathered_two, preferred_element_type=jnp.float32)
    logits = node_scale * (
        lax.psum_scatter(forward_two, "col", scatter_dimension=0, tiled=True)
        + source_two.astype(jnp.float32)
    )
    capped = SOFTCAP * jnp.tanh(logits / SOFTCAP)
    exp_capped = jnp.exp(capped)
    exp_total = jnp.sum(exp_capped, axis=1, keepdims=True)
    one_hot = (labels[:, None] == jnp.arange(capped.shape[1], dtype=jnp.int32)[None, :]).astype(
        jnp.float32
    )
    loss_local = jnp.sum(jnp.log(exp_total[:, 0]) - jnp.sum(capped * one_hot, axis=1))
    d_logits = (
        LOSS_SCALE
        / total_nodes
        * (exp_capped / exp_total - one_hot)
        * (1.0 - (capped / SOFTCAP) ** 2)
    )
    back_two = (node_scale * d_logits).astype(jnp.bfloat16)
    backward_two = lax.dot_general(
        adjacency, gather_targets(back_two), CONTRACT_ROWS, preferred_element_type=jnp.float32
    )
    d_source_two = node_scale * (sum_sources(backward_two) + back_two.astype(jnp.float32))
    grad_out_local = lax.dot_general(
        hidden.astype(jnp.float32), d_source_two, CONTRACT_ROWS, precision=HIGHEST
    )
    d_hidden = lax.dot_general(
        d_source_two, weight_out.astype(jnp.float32), (((1,), (1,)), ((), ())), precision=HIGHEST
    )
    back_one = (node_scale * jnp.where(pre_hidden > 0, d_hidden, 0.0)).astype(jnp.bfloat16)
    gathered_back = gather_targets(back_one)
    backward_one = lax.dot_general(
        adjacency, gathered_back, CONTRACT_ROWS, preferred_element_type=jnp.float32
    )
    d_source_one = sum_sources(backward_one) + back_one.astype(jnp.float32)
    grad_in_local = lax.dot_general(
        normed.astype(jnp.float32), d_source_one, CONTRACT_ROWS, precision=HIGHEST
    )
    grad_in, grad_out, loss_sum = lax.psum(
        (grad_in_local, grad_out_local, loss_local), ("row", "col")
    )
    return (grad_in, grad_out, loss_sum / total_nodes)


def solution(mesh):
    in_specs = (
        P(("row", "col"), None),
        P(("row", "col")),
        P(),
        P(),
        P(("row", "col")),
        P(("row", "col"), None),
        P(("row", "col"), None, None, None),
        P(("row", "col")),
    )
    out_specs = (P(), P(), P())
    return jax.shard_map(
        per_device, mesh=mesh, in_specs=in_specs, out_specs=out_specs, check_vma=False
    )
```

profile of v0, /device:TPU:0, one launch (start us, length us, event | category | flops | bytes accessed | tf_op | source)
XLA Modules:
  0.0 426.0 jit_solution(7901533714446784060)
XLA Ops:
  7.2 0.0 copy-start
  7.2 0.0 reduce-scatter.5.cloned.1.call-start
  7.2 1.7 fusion.37
  9.0 7.9 %iota_compare_fusion.17 = pred[128,512,128]{1,2,0:T(32,128)(4,1)} fusion(s32[128,512]{1,0:T(8,128)S(1)} %get-tuple-element.10), kind=kLoop, calls=%fused_computation.1.clone.clone.clone.clone.2 | loop fusion | flops 8388608 | bytes 8650752 | tf_op jit(solution)/shard_map/ser,sec->src/dot_general | solution.py:21
  17.6 0.0 copy-start.6
  17.6 14.4 %fusion.5 = bf16[128,128,128]{2,1,0:T(8,128)(2,1)S(1)} fusion(s32[128,512]{1,0:T(8,128)S(1)} %get-tuple-element.9, pred[128,512,128]{1,2,0:T(32,128)(4,1)} %iota_compare_fusion.17), kind=kOutput, calls=%fused_computation.8 | convolution fusion | flops 2157969408 | bytes 12845056 | tf_op jit(solution)/shard_map/ser,sec->src/dot_general | solution.py:21
  32.0 0.0 copy-start.4
  32.0 0.0 copy-start.2
  32.0 0.0 copy-start.3
  32.1 0.0 copy-done.6
  32.1 0.0 copy-start.5
  32.1 2.6 fusion.6
  34.7 0.2 copy.23
  34.9 0.7 copy.15
  35.7 0.1 copy.14
  35.8 0.2 fusion.34
  36.0 8.6 %all_gather.12 = f32[512,256]{1,0:T(8,128)S(1)} all-gather(f32[128,256]{1,0:T(8,128)S(1)} %fusion.34), channel_id=1, replica_groups=mesh['row'=4,'col'=8] {'row'}, dimensions={0}, use_global_device_ids=true | all-gather | bytes 655360 | tf_op jit(solution)/shard_map/all_gather | solution.py:58
  44.6 2.2 fusion.18
  46.8 0.0 reduce-scatter.5.cloned.1.call-update
  46.9 0.0 reduce-scatter.7.cloned.1.call-start
  46.9 64.4 %reduce-scatter.5.cloned.1.call-done = f32[128,256]{1,0:T(8,128)} async-done(((f32[1024,256]{1,0:T(8,128)}), f32[128,256]{1,0:T(8,128)}) %reduce-scatter.5.cloned.1.call-update) | async-done | bytes 131088 | tf_op jit(solution)/shard_map/reduce_scatter | solution.py:60
  111.3 1.2 fusion.11
  112.6 5.4 %all_gather.13 = bf16[512,128]{0,1:T(8,128)(2,1)S(1)} all-gather(bf16[128,128]{0,1:T(8,128)(2,1)S(1)} %fusion.11), channel_id=1, replica_groups=mesh['row'=4,'col'=8] {'row'}, dimensions={0}, use_global_device_ids=true | all-gather | bytes 163840 | tf_op jit(solution)/shard_map/all_gather | solution.py:66
  118.0 1.1 fusion.16
  119.1 0.0 reduce-scatter.7.cloned.1.call-update
  119.1 0.0 reduce-scatter.9.cloned.1.call-start
  119.2 61.5 %reduce-scatter.7.cloned.1.call-done = f32[128,128]{0,1:T(8,128)} async-done(((f32[1024,128]{0,1:T(8,128)}), f32[128,128]{0,1:T(8,128)}) %reduce-scatter.7.cloned.1.call-update) | async-done | bytes 65552 | tf_op jit(solution)/shard_map/reduce_scatter | solution.py:69
  180.7 0.9 select_reduce_fusion
  181.6 0.9 multiply_convert_fusion
  182.5 26.7 %all_gather.14 = bf16[1024,128]{0,1:T(8,128)(2,1)S(1)} all-gather(bf16[128,128]{0,1:T(8,128)(2,1)S(1)} %multiply_convert_fusion), channel_id=1, replica_groups=mesh['row'=4,'col'=8] {'col'}, dimensions={0}, use_global_device_ids=true | all-gather | bytes 294912 | tf_op jit(solution)/shard_map/all_gather | solution.py:38
  209.2 1.2 fusion.14
  210.3 0.0 reduce-scatter.9.cloned.1.call-update
  210.4 0.0 reduce-scatter.11.cloned.1.call-start
  210.4 17.7 %reduce-scatter.9.cloned.1.call-done = f32[128,128]{0,1:T(8,128)} async-done(((f32[512,128]{0,1:T(8,128)}), f32[128,128]{0,1:T(8,128)}) %reduce-scatter.9.cloned.1.call-update) | async-done | bytes 65552 | tf_op jit(solution)/shard_map/reduce_scatter | solution.py:42
  228.1 1.2 fusion.10
  229.3 31.4 %all_gather.15 = bf16[1024,256]{1,0:T(8,128)(2,1)S(1)} all-gather(bf16[128,256]{1,0:T(8,128)(2,1)S(1)} %fusion.10), channel_id=1, replica_groups=mesh['row'=4,'col'=8] {'col'}, dimensions={0}, use_global_device_ids=true | all-gather | bytes 589824 | tf_op jit(solution)/shard_map/all_gather | solution.py:38
  260.7 1.2 fusion.12
  262.0 0.0 reduce-scatter.11.cloned.1.call-update
  262.0 0.0 all-reduce.3.cloned.1.call-start
  262.0 1.8 fusion.29
  263.9 20.0 %reduce-scatter.11.cloned.1.call-done = f32[128,256]{1,0:T(8,128)} async-done(((f32[512,256]{1,0:T(8,128)}), f32[128,256]{1,0:T(8,128)}) %reduce-scatter.11.cloned.1.call-update) | async-done | bytes 131088 | tf_op jit(solution)/shard_map/reduce_scatter | solution.py:42
  283.8 1.8 fusion.24
  285.6 0.0 all-reduce.3.cloned.1.call-update
  285.7 0.6 subtract_reduce_fusion
  286.3 39.5 %psum.23 = f32[]{:T(128)} all-reduce(f32[]{:T(128)} %subtract_reduce_fusion), channel_id=1, replica_groups=mesh['row'=4,'col'=8] {'row','col'}, use_global_device_ids=true, to_apply=%region_9.10 | all-reduce | flops 1 | bytes 8 | tf_op jit(solution)/shard_map/psum | solution.py:105
  326.5 88.7 %all-reduce.3.cloned.1.call-done = (f32[128,256]{1,0:T(8,128)}, f32[256,128]{1,0:T(8,128)}) async-done(((f32[128,256]{1,0:T(8,128)}, f32[256,128]{1,0:T(8,128)}), (f32[128,256]{1,0:T(8,128)}, f32[256,128]{1,0:T(8,128)})) %all-reduce.3.cloned.1.call-update) | async-done | bytes 262160 | tf_op jit(solution)/shard_map/psum | solution.py:105
  415.2 1.6 copy.54
  416.7 1.6 copy.55
  (9 shorter events, 0.1 us)
Async XLA Ops:
  7.2 104.2 %copy-start = (bf16[256,128]{1,0:T(8,128)(2,1)S(1)}, bf16[256,128]{1,0:T(8,128)(2,1)}, u32[]{:S(2)}) copy-start(bf16[256,128]{1,0:T(8,128)(2,1)} %param.11) | copy-start | bytes 196612
  7.2 104.1 %reduce-scatter.5.cloned.1.call-start = ((), (), s32[]{:S(2)}) async-start(), calls=%async_computation.4 | async-start | bytes 1179648 | tf_op jit(solution)/shard_map/reduce_scatter | solution.py:60
  17.6 14.5 %copy-start.6 = (s32[1,128]{1,0:T(1,128)S(1)}, s32[1,128]{1,0:T(1,128)}, u32[]{:S(2)}) copy-start(s32[1,128]{1,0:T(1,128)} %param.13) | copy-start | bytes 1540
  32.0 3.6 copy-start.4
  32.0 3.7 copy-start.2
  32.0 3.7 copy-start.3
  32.1 148.6 %copy-start.5 = (s32[128]{0:T(128)S(1)}, s32[128]{0:T(128)}, u32[]{:S(2)}) copy-start(s32[128]{0:T(128)} %param.12) | copy-start | bytes 1540
  46.9 133.8 %reduce-scatter.7.cloned.1.call-start = ((), (), s32[]{:S(2)}) async-start(), calls=%async_computation.5 | async-start | bytes 589824 | tf_op jit(solution)/shard_map/reduce_scatter | solution.py:69
  111.3 150.7 %copy-start.1 = (f32[128,256]{1,0:T(8,128)S(1)}, f32[128,256]{1,0:T(8,128)}, u32[]{:S(2)}) copy-start(f32[128,256]{1,0:T(8,128)} %reduce-scatter.5.cloned.1.call-done) | copy-start | bytes 393220
  119.1 109.0 %reduce-scatter.9.cloned.1.call-start = ((), (), s32[]{:S(2)}) async-start(), calls=%async_computation.6 | async-start | bytes 327680 | tf_op jit(solution)/shard_map/reduce_scatter | solution.py:42
  210.4 73.5 %reduce-scatter.11.cloned.1.call-start = ((), (), s32[]{:S(2)}) async-start(), calls=%async_computation.7 | async-start | bytes 655360 | tf_op jit(solution)/shard_map/reduce_scatter | solution.py:42
  262.0 153.2 %all-reduce.3.cloned.1.call-start = ((), (), s32[]{:S(2)}) async-start(), calls=%async_computation.8 | async-start | bytes 524288 | tf_op jit(solution)/shard_map/psum | solution.py:105
Sparse Core Ops, SparseCore 0:
  47.0 64.3 reduce-scatter.4
  119.2 61.4 reduce-scatter.6
  210.5 17.5 reduce-scatter.8
  262.1 21.6 reduce-scatter.10
  289.9 125.1 all-reduce.2
where the time goes:
time: 426 us
  waiting for transfers between devices  252 us (59%)
  blocking collectives  112 us (26%)
  matrix products  29 us (7%)
  between operations  16.4 us (4%)
  other arithmetic  10.3 us (2%)
  local copies, waits for them, and re-layouts  6.02 us (1%)
    psum x1, waiting for transfers between devices, per_device(): lax.psum((grad_in_local, grad_out_local, loss_local), ('row', 'col'))  88.7 us
    reduce_scatter x1, waiting for transfers between devices, per_device(): lax.psum_scatter(forward_one, 'col', scatter_dimension=0, tiled=True)  64.4 us
    reduce_scatter x1, waiting for transfers between devices, per_device(): lax.psum_scatter(forward_two, 'col', scatter_dimension=0, tiled=True)  61.5 us
    all_gather x2, blocking collectives, gather_targets(): return lax.all_gather(values, 'col', axis=0, tiled=True)  58.1 us
    psum x1, blocking collectives, per_device(): lax.psum((grad_in_local, grad_out_local, loss_local), ('row', 'col'))  39.5 us
    reduce_scatter x2, waiting for transfers between devices, sum_sources(): lax.psum_scatter(partial_sums, 'row', scatter_dimension=0, tiled=True)  37.7 us
    dot_general x1, matrix products, densify(): jnp.einsum('ser,sec->src', row_onehot, col_onehot, preferred_element_type...  14.4 us
    all_gather x1, blocking collectives, per_device(): gathered_one = lax.all_gather(source_one, 'row', axis=0, tiled=True)  8.65 us
  transfers between devices with their start and end apart: 5, of which 5 were waited for; matrix products, arithmetic and copies ran while one was open for 1% of the time, Pallas kernels for 0%

commit v1 on v0

--- a/solution.py
+++ b/solution.py
@@ -103,7 +103,7 @@
         normed.astype(jnp.float32), d_source_one, CONTRACT_ROWS, precision=HIGHEST
     )
     grad_in, grad_out, loss_sum = lax.psum(
-        (grad_in_local, grad_out_local, loss_local), ("row", "col")
+        lax.psum((grad_in_local, grad_out_local, loss_local), "col"), "row"
     )
     return (grad_in, grad_out, loss_sum / total_nodes)
 

time: 426 us -> 404 us (0.948)
  blocking collectives: 112 us -> 98.6 us
  waiting for transfers between devices: 252 us -> 243 us
    psum x1 -> x2, blocking collectives: 39.5 us -> 26.6 us  [the longest x1 20.4 us: per_device(): lax.psum((grad_in_local, grad_out_local, loss_local), 'col')]
    psum x1 -> x2, waiting for transfers between devices: 88.7 us -> 78.8 us  [the longest x1 72.9 us: per_device(): lax.psum((grad_in_local, grad_out_local, loss_local), 'col')]
  transfers between devices with their start and end apart: 5 -> 6, of which waited for: 5 -> 6; matrix products, arithmetic and copies ran while one was open for 1% -> 1% of each run, Pallas kernels for 0% -> 0%
where the time goes in v1:
time: 404 us
  waiting for transfers between devices  243 us (60%)
  blocking collectives  98.6 us (24%)
  matrix products  29 us (7%)
  between operations  16.7 us (4%)
  other arithmetic  10.3 us (3%)
  local copies, waits for them, and re-layouts  6.02 us (1%)
    psum x1, waiting for transfers between devices, per_device(): lax.psum((grad_in_local, grad_out_local, loss_local), 'col')  72.9 us
    reduce_scatter x1, waiting for transfers between devices, per_device(): lax.psum_scatter(forward_one, 'col', scatter_dimension=0, tiled=True)  64.7 us
    reduce_scatter x1, waiting for transfers between devices, per_device(): lax.psum_scatter(forward_two, 'col', scatter_dimension=0, tiled=True)  61.6 us
    all_gather x2, blocking collectives, gather_targets(): return lax.all_gather(values, 'col', axis=0, tiled=True)  57.9 us
    reduce_scatter x2, waiting for transfers between devices, sum_sources(): lax.psum_scatter(partial_sums, 'row', scatter_dimension=0, tiled=True)  37.7 us
    psum x1, blocking collectives, per_device(): lax.psum((grad_in_local, grad_out_local, loss_local), 'col')  20.4 us
    dot_general x1, matrix products, densify(): jnp.einsum('ser,sec->src', row_onehot, col_onehot, preferred_element_type...  14.4 us
    all_gather x1, blocking collectives, per_device(): gathered_one = lax.all_gather(source_one, 'row', axis=0, tiled=True)  8.65 us
  transfers between devices with their start and end apart: 6, of which 6 were waited for; matrix products, arithmetic and copies ran while one was open for 1% of the time, Pallas kernels for 0%

profile of v1, /device:TPU:0, one launch (start us, length us, event | category | flops | bytes accessed | tf_op | source)
XLA Modules:
  0.0 403.6 jit_solution(15084742050495321334)
XLA Ops:
  7.2 0.0 copy-start
  7.2 0.0 reduce-scatter.5.cloned.1.call-start
  7.2 1.7 fusion.37
  9.0 7.9 %iota_compare_fusion.17 = pred[128,512,128]{1,2,0:T(32,128)(4,1)} fusion(s32[128,512]{1,0:T(8,128)S(1)} %get-tuple-element.12), kind=kLoop, calls=%fused_computation.1.clone.clone.clone.clone.2 | loop fusion | flops 8388608 | bytes 8650752 | tf_op jit(solution)/shard_map/ser,sec->src/dot_general | solution.py:21
  17.6 14.4 %fusion.5 = bf16[128,128,128]{2,1,0:T(8,128)(2,1)S(1)} fusion(s32[128,512]{1,0:T(8,128)S(1)} %get-tuple-element.11, pred[128,512,128]{1,2,0:T(32,128)(4,1)} %iota_compare_fusion.17), kind=kOutput, calls=%fused_computation.8 | convolution fusion | flops 2157969408 | bytes 12845056 | tf_op jit(solution)/shard_map/ser,sec->src/dot_general | solution.py:21
  32.0 0.0 copy-start.4
  32.1 0.0 copy-start.5
  32.1 2.6 fusion.6
  34.7 0.2 copy.23
  34.9 0.7 copy.15
  35.7 0.1 copy.14
  35.8 0.2 fusion.34
  36.0 8.6 %all_gather.12 = f32[512,256]{1,0:T(8,128)S(1)} all-gather(f32[128,256]{1,0:T(8,128)S(1)} %fusion.34), channel_id=1, replica_groups=mesh['row'=4,'col'=8] {'row'}, dimensions={0}, use_global_device_ids=true | all-gather | bytes 655360 | tf_op jit(solution)/shard_map/all_gather | solution.py:58
  44.6 2.2 fusion.18
  46.8 0.0 reduce-scatter.5.cloned.1.call-update
  46.9 0.0 reduce-scatter.7.cloned.1.call-start
  46.9 64.7 %reduce-scatter.5.cloned.1.call-done = f32[128,256]{1,0:T(8,128)} async-done(((f32[1024,256]{1,0:T(8,128)}), f32[128,256]{1,0:T(8,128)}) %reduce-scatter.5.cloned.1.call-update) | async-done | bytes 131088 | tf_op jit(solution)/shard_map/reduce_scatter | solution.py:60
  111.6 1.2 fusion.11
  112.8 5.4 %all_gather.13 = bf16[512,128]{0,1:T(8,128)(2,1)S(1)} all-gather(bf16[128,128]{0,1:T(8,128)(2,1)S(1)} %fusion.11), channel_id=1, replica_groups=mesh['row'=4,'col'=8] {'row'}, dimensions={0}, use_global_device_ids=true | all-gather | bytes 163840 | tf_op jit(solution)/shard_map/all_gather | solution.py:66
  118.3 1.1 fusion.16
  119.4 0.0 reduce-scatter.7.cloned.1.call-update
  119.4 0.0 reduce-scatter.9.cloned.1.call-start
  119.5 61.6 %reduce-scatter.7.cloned.1.call-done = f32[128,128]{0,1:T(8,128)} async-done(((f32[1024,128]{0,1:T(8,128)}), f32[128,128]{0,1:T(8,128)}) %reduce-scatter.7.cloned.1.call-update) | async-done | bytes 65552 | tf_op jit(solution)/shard_map/reduce_scatter | solution.py:69
  181.0 0.9 select_reduce_fusion
  181.9 0.9 multiply_convert_fusion
  182.8 26.5 %all_gather.14 = bf16[1024,128]{0,1:T(8,128)(2,1)S(1)} all-gather(bf16[128,128]{0,1:T(8,128)(2,1)S(1)} %multiply_convert_fusion), channel_id=1, replica_groups=mesh['row'=4,'col'=8] {'col'}, dimensions={0}, use_global_device_ids=true | all-gather | bytes 294912 | tf_op jit(solution)/shard_map/all_gather | solution.py:38
  209.3 1.2 fusion.14
  210.5 0.0 reduce-scatter.9.cloned.1.call-update
  210.5 0.0 reduce-scatter.11.cloned.1.call-start
  210.6 17.7 %reduce-scatter.9.cloned.1.call-done = f32[128,128]{0,1:T(8,128)} async-done(((f32[512,128]{0,1:T(8,128)}), f32[128,128]{0,1:T(8,128)}) %reduce-scatter.9.cloned.1.call-update) | async-done | bytes 65552 | tf_op jit(solution)/shard_map/reduce_scatter | solution.py:42
  228.3 1.2 fusion.10
  229.5 31.4 %all_gather.15 = bf16[1024,256]{1,0:T(8,128)(2,1)S(1)} all-gather(bf16[128,256]{1,0:T(8,128)(2,1)S(1)} %fusion.10), channel_id=1, replica_groups=mesh['row'=4,'col'=8] {'col'}, dimensions={0}, use_global_device_ids=true | all-gather | bytes 589824 | tf_op jit(solution)/shard_map/all_gather | solution.py:38
  260.9 1.2 fusion.12
  262.1 0.0 reduce-scatter.11.cloned.1.call-update
  262.1 0.0 all-reduce.5.cloned.1.call-start
  262.2 1.8 fusion.29
  264.0 20.0 %reduce-scatter.11.cloned.1.call-done = f32[128,256]{1,0:T(8,128)} async-done(((f32[512,256]{1,0:T(8,128)}), f32[128,256]{1,0:T(8,128)}) %reduce-scatter.11.cloned.1.call-update) | async-done | bytes 131088 | tf_op jit(solution)/shard_map/reduce_scatter | solution.py:42
  284.0 1.8 fusion.24
  285.8 0.0 all-reduce.5.cloned.1.call-update
  285.8 0.0 all-reduce.7.cloned.1.call-start
  285.8 72.9 %all-reduce.5.cloned.1.call-done = (f32[128,256]{1,0:T(8,128)}, f32[256,128]{1,0:T(8,128)}) async-done(((f32[128,256]{1,0:T(8,128)}, f32[256,128]{1,0:T(8,128)}), (f32[128,256]{1,0:T(8,128)}, f32[256,128]{1,0:T(8,128)})) %all-reduce.5.cloned.1.call-update) | async-done | bytes 262160 | tf_op jit(solution)/shard_map/psum | solution.py:106
  358.7 0.0 all-reduce.7.cloned.1.call-update
  358.8 0.6 subtract_reduce_fusion
  359.4 20.4 %psum.46 = f32[]{:T(128)} all-reduce(f32[]{:T(128)} %subtract_reduce_fusion), channel_id=1, replica_groups=mesh['row'=4,'col'=8] {'col'}, use_global_device_ids=true, to_apply=%region_11.12 | all-reduce | flops 1 | bytes 8 | tf_op jit(solution)/shard_map/psum | solution.py:106
  379.7 6.3 %psum.47 = f32[]{:T(128)} all-reduce(f32[]{:T(128)} %psum.46), channel_id=1, replica_groups=mesh['row'=4,'col'=8] {'row'}, use_global_device_ids=true, to_apply=%region_12.13 | all-reduce | flops 1 | bytes 8 | tf_op jit(solution)/shard_map/psum | solution.py:105
  386.7 5.9 %all-reduce.7.cloned.1.call-done = (f32[128,256]{1,0:T(8,128)}, f32[256,128]{1,0:T(8,128)}) async-done(((f32[128,256]{1,0:T(8,128)}, f32[256,128]{1,0:T(8,128)}), (f32[128,256]{1,0:T(8,128)}, f32[256,128]{1,0:T(8,128)})) %all-reduce.7.cloned.1.call-update) | async-done | bytes 262160 | tf_op jit(solution)/shard_map/psum | solution.py:105
  392.5 1.6 copy.56
  394.1 1.6 copy.57
  (13 shorter events, 0.1 us)
Async XLA Ops:
  7.2 104.5 %copy-start = (bf16[256,128]{1,0:T(8,128)(2,1)S(1)}, bf16[256,128]{1,0:T(8,128)(2,1)}, u32[]{:S(2)}) copy-start(bf16[256,128]{1,0:T(8,128)(2,1)} %param.11) | copy-start | bytes 196612
  7.2 104.4 %reduce-scatter.5.cloned.1.call-start = ((), (), s32[]{:S(2)}) async-start(), calls=%async_computation.4 | async-start | bytes 1179648 | tf_op jit(solution)/shard_map/reduce_scatter | solution.py:60
  17.6 14.5 %copy-start.6 = (s32[1,128]{1,0:T(1,128)S(1)}, s32[1,128]{1,0:T(1,128)}, u32[]{:S(2)}) copy-start(s32[1,128]{1,0:T(1,128)} %param.13) | copy-start | bytes 1540
  32.0 3.6 copy-start.4
  32.0 3.7 copy-start.2
  32.0 3.7 copy-start.3
  32.1 149.0 %copy-start.5 = (s32[128]{0:T(128)S(1)}, s32[128]{0:T(128)}, u32[]{:S(2)}) copy-start(s32[128]{0:T(128)} %param.12) | copy-start | bytes 1540
  46.9 134.2 %reduce-scatter.7.cloned.1.call-start = ((), (), s32[]{:S(2)}) async-start(), calls=%async_computation.5 | async-start | bytes 589824 | tf_op jit(solution)/shard_map/reduce_scatter | solution.py:69
  111.6 150.5 %copy-start.1 = (f32[128,256]{1,0:T(8,128)S(1)}, f32[128,256]{1,0:T(8,128)}, u32[]{:S(2)}) copy-start(f32[128,256]{1,0:T(8,128)} %reduce-scatter.5.cloned.1.call-done) | copy-start | bytes 393220
  119.4 108.9 %reduce-scatter.9.cloned.1.call-start = ((), (), s32[]{:S(2)}) async-start(), calls=%async_computation.6 | async-start | bytes 327680 | tf_op jit(solution)/shard_map/reduce_scatter | solution.py:42
  210.5 73.5 %reduce-scatter.11.cloned.1.call-start = ((), (), s32[]{:S(2)}) async-start(), calls=%async_computation.7 | async-start | bytes 655360 | tf_op jit(solution)/shard_map/reduce_scatter | solution.py:42
  262.1 96.6 %all-reduce.5.cloned.1.call-start = ((), (), s32[]{:S(2)}) async-start(), calls=%async_computation.8 | async-start | bytes 524288 | tf_op jit(solution)/shard_map/psum | solution.py:106
  285.8 106.7 %all-reduce.7.cloned.1.call-start = ((), (), s32[]{:S(2)}) async-start(), calls=%async_computation.9 | async-start | bytes 524288 | tf_op jit(solution)/shard_map/psum | solution.py:105
Sparse Core Ops, SparseCore 0:
  47.0 64.5 reduce-scatter.4
  119.5 61.4 reduce-scatter.6
  210.6 17.5 reduce-scatter.8
  262.2 21.6 reduce-scatter.10
  287.9 70.8 all-reduce.4
  361.1 31.3 all-reduce.6
